TPU v7x, 128 devices: a whole 4x4x4 slice. The times are simulated.
128 devices in a mesh: expert: 8 (over x_lo, y), fsdp: 16 (over z, x_hi, core).
Axes of the slice: x: 4 (x_hi: 2, x_lo: 2; x = x_hi * 2 + x_lo), y: 4, z: 4, core: 2. Of those that a mesh axis runs over, the one named last changes fastest.
Arguments:
- tokens: bfloat16 [8192, 3072], P(('expert', 'fsdp')), may hold values from -6 to 6
- expert_ids: int32 [8192, 2], P(('expert', 'fsdp')), may hold values from 0 to 7, all different within a row; in each aligned block of 64 rows (0 to 63, 64 to 127, ...) at most 18 rows name the same one
- route_weights: float32 [8192, 2], P(('expert', 'fsdp')), may hold values from 0.2 to 1
- up_weight: bfloat16 [8, 16384, 3072], P('expert', 'fsdp'), may hold values from -0.109375 to 0.109375
- down_weight: bfloat16 [8, 16384, 3072], P('expert', 'fsdp'), may hold values from -0.046875 to 0.046875
Outputs:
- mixed: bfloat16 [8192, 3072], P(('expert', 'fsdp'))
Inputs may be any that keep to these rules, and one draw needn't show every extreme that they name: `expert_ids`: each row names 2 different experts. Within the rows of one device (aligned blocks of 64 rows) no expert is named by more than 18 rows, and in every block some expert is named by exactly 18 rows.
All inputs are finite; a program needn't handle non-finite values.
Results may differ from a plain program's by a relative error of at most 0.019.
Values may be sent and summed in bfloat16 or wider, within the bound.
A program may use at most 128 MiB of HBM per device.

v0:
```python
import jax
import jax.numpy as jnp
from jax import lax
from jax.sharding import PartitionSpec as P


def shards(tokens, expert_ids, route_weights, up_weight, down_weight):
    experts = lax.axis_size("expert")
    tok_rows, features = tokens.shape
    top_count = expert_ids.shape[1]
    capacity = tok_rows * top_count * 9 // (8 * experts)
    numbers = jnp.arange(experts, dtype=jnp.int32)
    chosen = (expert_ids[:, :, None] == numbers).astype(jnp.int32)
    counts = chosen.sum(1)
    before = jnp.cumsum(counts, axis=0) - counts
    slot_index = jnp.sum(chosen * before[:, None, :], axis=2)
    target = expert_ids * capacity + slot_index
    places = jnp.arange(experts * capacity, dtype=jnp.int32)
    onehot = jnp.any(places[:, None, None] == target[None], axis=2).astype(jnp.bfloat16)
    outgoing = jnp.dot(onehot, tokens, preferred_element_type=jnp.float32).astype(jnp.bfloat16)
    outgoing = outgoing.reshape(experts, capacity, features)
    up_panel = up_weight[0]
    down_panel = down_weight[0]
    received = lax.all_to_all(outgoing, "expert", split_axis=0, concat_axis=0, tiled=True)
    source_count, slot_count, _ = received.shape
    flat_rows = received.reshape(source_count * slot_count, features)
    hidden = jax.nn.silu(
        lax.dot_general(
            lax.all_gather(flat_rows, "fsdp", axis=0, tiled=True),
            up_panel,
            (((1,), (1,)), ((), ())),
            preferred_element_type=jnp.float32,
        )
    ).astype(jnp.bfloat16)
    summed = lax.psum_scatter(
        jnp.dot(hidden, down_panel, preferred_element_type=jnp.float32).astype(jnp.bfloat16),
        "fsdp",
        scatter_dimension=0,
        tiled=True,
    )
    returned = lax.all_to_all(
        summed.reshape(source_count, slot_count, features),
        "expert",
        split_axis=0,
        concat_axis=0,
        tiled=True,
    )
    flattened = returned.reshape(experts * capacity, features)
    picked = flattened[target]
    combined = jnp.sum(route_weights[:, :, None] * picked.astype(jnp.float32), axis=1)
    return combined.astype(jnp.bfloat16)


def solution(mesh):
    return jax.shard_map(
        shards,
        mesh=mesh,
        in_specs=(
            P(("expert", "fsdp"), None),
            P(("expert", "fsdp"), None),
            P(("expert", "fsdp"), None),
            P("expert", "fsdp", None),
            P("expert", "fsdp", None),
        ),
        out_specs=P(("expert", "fsdp"), None),
        check_vma=False,
    )
```

profile of v0, /device:TPU:0, one launch (start us, length us, event | category | flops | bytes accessed | tf_op | source)
XLA Modules:
  0.0 333.7 jit_solution(1554929253555458984)
XLA Ops:
  6.5 0.0 copy-start
  6.5 0.0 all-gather.2.cloned.1.call-start
  6.5 0.7 convert_reduce_fusion
  7.3 0.1 copy.15
  7.4 0.1 reduce_window_sum.11
  7.5 0.1 copy.17
  7.5 0.7 select_reduce_fusion
  8.2 0.7 compare_select_fusion
  8.9 0.1 fusion.5
  9.0 0.0 copy-done
  9.0 0.4 convolution_convert_fusion.1
  9.5 0.3 reshape.24
  9.7 22.5 %all_to_all.10 = bf16[8,18,3072]{2,1,0:T(8,128)(2,1)S(1)} all-to-all(bf16[8,18,3072]{2,1,0:T(8,128)(2,1)S(1)} %reshape.24), channel_id=1, replica_groups=mesh['expert'=8,'fsdp'=16] {'expert'}, dimensions={0} | all-to-all | bytes 1769472 | tf_op jit(solution)/shard_map/all_to_all | solution.py:24
  32.2 1.2 reshape.25
  33.5 0.0 all-gather.2.cloned.1.call-update
  33.5 0.0 reduce-scatter.2.cloned.1.call-start
  33.5 97.7 %all-gather.2.cloned.1.call-done = bf16[2304,3072]{1,0:T(8,128)(2,1)} async-done(((bf16[144,3072]{1,0:T(8,128)(2,1)}), bf16[2304,3072]{1,0:T(8,128)(2,1)}) %all-gather.2.cloned.1.call-update) | async-done | bytes 14155792 | tf_op jit(solution)/shard_map/all_gather | solution.py:29
  131.2 20.5 %multiply_convert_fusion = bf16[2304,1024]{1,0:T(8,128)(2,1)S(1)} fusion(bf16[2304,3072]{1,0:T(8,128)(2,1)} %all-gather.2.cloned.1.call-done, bf16[1,1024,3072]{2,1,0:T(8,128)(2,1)} %param.8), kind=kOutput, calls=%fused_computation.2 | convolution fusion | flops 14507311104 | bytes 25165824 | tf_op jit(solution)/shard_map/dot_general | solution.py:28
  151.7 20.0 %convolution_convert_fusion = bf16[2304,3072]{1,0:T(8,128)(2,1)} fusion(bf16[2304,1024]{1,0:T(8,128)(2,1)S(1)} %multiply_convert_fusion, bf16[1,1024,3072]{2,1,0:T(8,128)(2,1)} %param.9), kind=kOutput, calls=%fused_computation.1 | convolution fusion | flops 14502592512 | bytes 25165824 | tf_op jit(solution)/shard_map/dot_general | solution.py:36
  171.8 0.0 reduce-scatter.2.cloned.1.call-update
  171.8 127.5 %reduce-scatter.2.cloned.1.call-done = bf16[144,3072]{1,0:T(8,128)(2,1)} async-done(((bf16[2304,3072]{1,0:T(8,128)(2,1)}), bf16[144,3072]{1,0:T(8,128)(2,1)}) %reduce-scatter.2.cloned.1.call-update) | async-done | bytes 884752 | tf_op jit(solution)/shard_map/reduce_scatter | solution.py:35
  299.3 2.4 reshape.26
  301.7 4.3 %all-to-all-start.1 = ((bf16[8,18,3072]{2,1,0:T(8,128)(2,1)}), bf16[8,18,3072]{2,1,0:T(8,128)(2,1)S(1)}, u32[]{:S(2)}, u32[]{:S(2)}) async-start(bf16[8,18,3072]{2,1,0:T(8,128)(2,1)} %reshape.26), calls=%async_computation.2 | async-start | bytes 2359296 | tf_op jit(solution)/shard_map/all_to_all | solution.py:41
  306.1 0.1 copy.18
  306.2 0.1 reshape.30
  306.3 0.0 copy-done.1
  306.3 0.1 copy.14
  306.4 15.2 %all-to-all-done.1 = bf16[8,18,3072]{2,1,0:T(8,128)(2,1)S(1)} async-done(((bf16[8,18,3072]{2,1,0:T(8,128)(2,1)}), bf16[8,18,3072]{2,1,0:T(8,128)(2,1)S(1)}, u32[]{:S(2)}, u32[]{:S(2)}) %all-to-all-start.1) | async-done | bytes 884768 | tf_op jit(solution)/shard_map/all_to_all | solution.py:41
  321.7 0.3 reshape.27
  321.9 1.0 gather_fusion
  323.0 1.0 reshape.38
  323.9 2.9 multiply_reduce_fusion
  (3 shorter events, 0.0 us)
Async XLA Ops:
  6.5 2.5 copy-start
  6.5 124.7 %all-gather.2.cloned.1.call-start = ((), (), s32[]{:S(2)}) async-start(), calls=%async_computation.3 | async-start | bytes 15040512 | tf_op jit(solution)/shard_map/all_gather | solution.py:29
  33.5 265.8 %reduce-scatter.2.cloned.1.call-start = ((), (), s32[]{:S(2)}) async-start(), calls=%async_computation.4 | async-start | bytes 15040512 | tf_op jit(solution)/shard_map/reduce_scatter | solution.py:35
  171.8 134.5 %copy-start.1 = (f32[64,2]{0,1:T(2,128)S(1)}, f32[64,2]{0,1:T(2,128)}, u32[]{:S(2)}) copy-start(f32[64,2]{0,1:T(2,128)} %param.7) | copy-start | bytes 1540
  301.7 19.9 %all-to-all-start.1 = ((bf16[8,18,3072]{2,1,0:T(8,128)(2,1)}), bf16[8,18,3072]{2,1,0:T(8,128)(2,1)S(1)}, u32[]{:S(2)}, u32[]{:S(2)}) async-start(bf16[8,18,3072]{2,1,0:T(8,128)(2,1)} %reshape.26), calls=%async_computation.2 | async-start | bytes 2359296 | tf_op jit(solution)/shard_map/all_to_all | solution.py:41
Sparse Core Ops, SparseCore 0:
  33.6 97.5 all-gather.1
  171.9 127.3 reduce-scatter.1
where the time goes:
time: 335 us; the launch traced here: 334 us
  waiting for transfers between devices  240 us (72%)
  matrix products  41 us (12%)
  blocking collectives  22.5 us (7%)
  between operations  13.5 us (4%)
  local copies, waits for them, and re-layouts  6.66 us (2%)
  other arithmetic  5.25 us (2%)
  starting transfers between devices  4.36 us (1%)
    reduce_scatter x1, waiting for transfers between devices, shards(): lax.psum_scatter(jnp.dot(hidden, down_panel, preferred_element_type=jnp.f...  128 us
    all_gather x1, waiting for transfers between devices, shards(): lax.all_gather(flat_rows, 'fsdp', axis=0, tiled=True)  97.7 us
    all_to_all x1, blocking collectives, shards(): lax.all_to_all(outgoing, 'expert', split_axis=0, concat_axis=0, tiled=True)  22.5 us
    dot_general x1, matrix products, shards(): lax.dot_general(lax.all_gather(flat_rows, 'fsdp', axis=0, tiled=True), up...  20.5 us
    dot_general x1, matrix products, shards(): jnp.dot(hidden, down_panel, preferred_element_type=jnp.float32)  20 us
    all_to_all x1, waiting for transfers between devices, shards(): lax.all_to_all(summed.reshape(source_count, slot_count, features), 'exper...  15.2 us
  transfers between devices with their start and end apart: 3, of which 3 were waited for; matrix products, arithmetic and copies ran while one was open for 0% of the time, Pallas kernels for 0%

commit v1 on v0

v1 whole, which is shorter than its diff:
```python
import functools

import jax
import jax.numpy as jnp
from jax import lax
from jax.experimental import pallas as pl
from jax.experimental.pallas import tpu as pltpu
from jax.sharding import PartitionSpec as P

MESH = pl.DeviceIdType.MESH
BF16, F32 = jnp.bfloat16, jnp.float32

OFFSETS = (
    (0, 0), (1, 0), (3, 0), (0, 1),
    (0, 3), (2, 0), (0, 2), (1, 1),
    (3, 3), (1, 3), (3, 1), (2, 1),
    (1, 2), (2, 3), (3, 2), (2, 2),
)
PEERS = len(OFFSETS)
TILE = 16
EXTRA = 2
GROUPS = TILE // EXTRA
PIECES = 4
PIECE = PEERS // PIECES * TILE
PLANE = PEERS * TILE
REST = PEERS * EXTRA
ROWS = PLANE + REST
TILE_N = 256
WAY_A, WAY_B = (0, 1), (2, 3)


def iota(shape, dim):
    return lax.broadcasted_iota(jnp.int32, shape, dim)


def onehot(mask):
    return jnp.where(mask, 1.0, 0.0).astype(BF16)


def kernel(
    tok_ref, ids_ref, rw_ref, up_ref, down_ref, out_ref,
    up_v, down_v, x_v, y_v, from_up, from_down, far_v, back_v, send_v, hid_v, perm_v, permt_v,
    sem_w, sem_ws, sem_wr, sem_self, sem_ps, sem_pr, sem_as, sem_ar, sem_fs, sem_fr,
    sem_2s, sem_2r, sem_1s, sem_1r, sem_bs, sem_br,
):
    tok_rows, features = tok_ref.shape
    units = up_ref.shape[0]
    fold = features // GROUPS
    e, f = lax.axis_index("expert"), lax.axis_index("fsdp")
    x_lo, y = e // 4, e % 4
    z, x_hi, core = f // 4, (f // 2) % 2, f % 2
    x = x_hi * 2 + x_lo

    def device(dx, dy, dz=0, dc=0):
        px, py, pz, pc = (x + dx) % 4, (y + dy) % 4, (z + dz) % 4, (core + dc) % 2
        return {"expert": (px % 2) * 4 + py, "fsdp": (pz * 2 + px // 2) * 2 + pc}

    peers = [device(dx, dy) for dx, dy in OFFSETS]
    backs = [device(-dx, -dy) for dx, dy in OFFSETS]
    above, below, twin = device(0, 0, 1), device(0, 0, -1), device(0, 0, 0, 1)

    barrier = pltpu.get_barrier_semaphore()
    greeted = peers[1:] + [above, below, twin]
    for other in greeted:
        pl.semaphore_signal(barrier, inc=1, device_id=other, device_id_type=MESH)

    own_up = pltpu.make_async_copy(up_ref, up_v.at[pl.ds(0, units)], sem_w.at[0])
    own_down = pltpu.make_async_copy(down_ref, down_v.at[pl.ds(0, units)], sem_w.at[1])
    own_up.start()
    own_down.start()

    ids = ids_ref[...]
    id0, id1 = ids[:, 0:1], ids[:, 1:2]
    lanes = iota((tok_rows, 128), 1)
    chosen = onehot((id0 == lanes) | (id1 == lanes))
    earlier = onehot(iota((tok_rows, tok_rows), 1) < iota((tok_rows, tok_rows), 0))
    before = jnp.dot(earlier, chosen, preferred_element_type=F32)
    slot0 = jnp.sum(jnp.where(id0 == lanes, before, 0.0), axis=1, keepdims=True).astype(jnp.int32)
    slot1 = jnp.sum(jnp.where(id1 == lanes, before, 0.0), axis=1, keepdims=True).astype(jnp.int32)

    blocks = 8
    wide = blocks * TILE
    place = iota((tok_rows, wide), 1)
    block, within = place // TILE, place % TILE
    expert_of = ((x + block // 4) % 2) * 4 + (y + block % 4) % 4
    in0, in1 = id0 == expert_of, id1 == expert_of
    pick_main = onehot((in0 & (slot0 == within)) | (in1 & (slot1 == within)))
    last = TILE + within % EXTRA
    pick_extra = (in0 & (slot0 == last)) | (in1 & (slot1 == last))
    tokens = tok_ref[...]
    rows_first = (((0,), (0,)), ((), ()))
    send_v[:, :features] = lax.dot_general(pick_main, tokens, rows_first, preferred_element_type=F32).astype(BF16)
    extra = jnp.zeros((wide, fold), F32)
    for g in range(GROUPS):
        extra += lax.dot_general(
            onehot(pick_extra & (within // EXTRA == g)), tok_ref[:, g * fold:(g + 1) * fold],
            rows_first, preferred_element_type=F32)
    send_v[:, features:] = extra.astype(BF16)

    pl.semaphore_wait(barrier, len(greeted))

    def block_of(r):
        dx, dy = OFFSETS[r]
        return (dx % 2) * 4 + dy

    keep = pltpu.make_async_copy(send_v.at[pl.ds(0, TILE)], x_v.at[0, pl.ds(0, TILE)], sem_self.at[0])
    keep.start()
    out_copies = [
        pltpu.make_async_remote_copy(
            src_ref=send_v.at[pl.ds(block_of(r) * TILE, TILE)], dst_ref=x_v.at[0, pl.ds(r * TILE, TILE)],
            send_sem=sem_ps.at[r], recv_sem=sem_pr.at[r], device_id=peers[r], device_id_type=MESH)
        for r in range(1, PEERS)
    ]
    for copy in out_copies:
        copy.start()

    twin_copies = [
        pltpu.make_async_remote_copy(
            src_ref=src, dst_ref=dst.at[pl.ds(units, units)], send_sem=sem_ws.at[i], recv_sem=sem_wr.at[i],
            device_id=twin, device_id_type=MESH)
        for i, (src, dst) in enumerate(((up_ref, up_v), (down_ref, down_v)))
    ]
    for copy in twin_copies:
        copy.start()

    out_row, in_row = iota((PLANE, PLANE), 0), iota((PLANE, PLANE), 1)
    perm_v[...] = onehot(in_row == (out_row % REST) // EXTRA * TILE + out_row // REST * EXTRA + out_row % EXTRA)
    permt_v[...] = onehot(out_row == (in_row % REST) // EXTRA * TILE + in_row // REST * EXTRA + in_row % EXTRA)

    def piece(k):
        return pl.ds(k * PIECE, PIECE)

    def link(src, dst, send, recv, to):
        return pltpu.make_async_remote_copy(
            src_ref=src, dst_ref=dst, send_sem=send, recv_sem=recv, device_id=to, device_id_type=MESH)

    up_copies = [link(x_v.at[0, piece(k)], x_v.at[3, piece(k)], sem_as.at[0, k], sem_ar.at[0, k], above) for k in range(PIECES)]
    down_copies = [link(x_v.at[0, piece(k)], x_v.at[1, piece(k)], sem_as.at[1, k], sem_ar.at[1, k], below) for k in range(PIECES)]
    on_up = [link(x_v.at[3, piece(k)], x_v.at[2, piece(k)], sem_fs.at[k], sem_fr.at[k], above) for k in WAY_A]
    on_down = [link(x_v.at[1, piece(k)], x_v.at[2, piece(k)], sem_fs.at[k], sem_fr.at[k], below) for k in WAY_B]

    for k in range(PIECES):
        for r in range(k * PEERS // PIECES, (k + 1) * PEERS // PIECES):
            if r == 0:
                keep.wait()
            else:
                out_copies[r - 1].wait_recv()
        up_copies[k].start()
        down_copies[k].start()

    def unfold(j):
        moved = jnp.dot(perm_v[...], x_v[j, 0:PLANE, features:], preferred_element_type=F32).astype(BF16)
        for g in range(GROUPS):
            x_v[j, PLANE:ROWS, g * fold:(g + 1) * fold] = moved[g * REST:(g + 1) * REST]

    def refold(j):
        total = jnp.zeros((PLANE, fold), F32)
        for g in range(GROUPS):
            total += jnp.dot(permt_v[:, g * REST:(g + 1) * REST], y_v[j, PLANE:ROWS, g * fold:(g + 1) * fold],
                             preferred_element_type=F32)
        y_v[j, 0:PLANE, features:] = total.astype(BF16)

    def into_hidden(j, first, count):
        def body(n, carry):
            at = pl.ds(pl.multiple_of(n * TILE_N, TILE_N), TILE_N)
            v = lax.dot_general(x_v[j, :, :features], up_v[at, :], (((1,), (1,)), ((), ())), preferred_element_type=F32)
            hid_v[:, at] = (v / (1.0 + jnp.exp(-v))).astype(BF16)
            return carry

        lax.fori_loop(first // TILE_N, (first + count) // TILE_N, body, 0)

    def out_of_hidden(j):
        def body(n, carry):
            at = pl.ds(pl.multiple_of(n * TILE_N, TILE_N), TILE_N)
            y_v[j, :, at] = jnp.dot(hid_v[...], down_v[:, at], preferred_element_type=F32).astype(BF16)
            return carry

        lax.fori_loop(0, features // TILE_N, body, 0)

    unfold(0)
    own_up.wait()
    into_hidden(0, 0, units)
    twin_copies[0].wait_recv()
    into_hidden(0, units, units)
    own_down.wait()
    twin_copies[1].wait_recv()
    out_of_hidden(0)
    refold(0)

    for i in range(len(WAY_A)):
        up_copies[WAY_A[i]].wait_recv()
        on_up[i].start()
    for k in range(PIECES):
        down_copies[k].wait_recv()
        if k in WAY_B:
            on_down[WAY_B.index(k)].start()
    for k in WAY_B:
        up_copies[k].wait_recv()

    to_above = [link(y_v.at[1, piece(k)], from_down.at[piece(k)], sem_1s.at[0, k], sem_1r.at[0, k], above) for k in range(PIECES)]
    to_below = [link(y_v.at[3, piece(k)], from_up.at[piece(k)], sem_1s.at[1, k], sem_1r.at[1, k], below) for k in range(PIECES)]
    far_below = [link(y_v.at[2, piece(k)], far_v.at[piece(k)], sem_2s.at[k], sem_2r.at[k], below) for k in WAY_A]
    far_above = [link(y_v.at[2, piece(k)], far_v.at[piece(k)], sem_2s.at[k], sem_2r.at[k], above) for k in WAY_B]

    def whole(j):
        unfold(j)
        into_hidden(j, 0, 2 * units)
        out_of_hidden(j)
        refold(j)

    whole(1)
    for k in WAY_A:
        to_above[k].start()
    whole(3)
    for k in WAY_B:
        to_below[k].start()
    for copy in on_up + on_down:
        copy.wait_recv()
    whole(2)
    for copy in far_below + far_above:
        copy.start()

    def add_into(target, j, k, others):
        total = target[j, piece(k), :].astype(F32)
        for other in others:
            total += other[piece(k), :].astype(F32)
        target[j, piece(k), :] = total.astype(BF16)

    for i in range(len(WAY_A)):
        far_below[i].wait_recv()
        add_into(y_v, 3, WAY_A[i], (far_v,))
        to_below[WAY_A[i]].start()
        far_above[i].wait_recv()
        add_into(y_v, 1, WAY_B[i], (far_v,))
        to_above[WAY_B[i]].start()

    back_keep = pltpu.make_async_copy(y_v.at[0, pl.ds(0, TILE)], back_v.at[pl.ds(0, TILE)], sem_self.at[1])
    back_copies = [
        link(y_v.at[0, pl.ds(r * TILE, TILE)], back_v.at[pl.ds(r * TILE, TILE)], sem_bs.at[r], sem_br.at[r], backs[r])
        for r in range(1, PEERS)
    ]
    for k in (0, 2, 1, 3):
        to_above[k].wait_recv()
        to_below[k].wait_recv()
        add_into(y_v, 0, k, (from_up, from_down))
        for r in range(k * PEERS // PIECES, (k + 1) * PEERS // PIECES):
            (back_keep if r == 0 else back_copies[r - 1]).start()

    rw = rw_ref[...]
    w0, w1 = rw[:, 0:1], rw[:, 1:2]
    place = iota((tok_rows, PLANE), 1)
    block, within = place // TILE, place % TILE
    dx, dy = jnp.zeros_like(place), jnp.zeros_like(place)
    for r, (rx, ry) in enumerate(OFFSETS):
        dx, dy = jnp.where(block == r, rx, dx), jnp.where(block == r, ry, dy)
    expert_of = ((x + dx) % 2) * 4 + (y + dy) % 4
    in0, in1 = id0 == expert_of, id1 == expert_of

    def weigh(slot):
        full = jnp.where(in0 & (slot0 == slot), w0, 0.0) + jnp.where(in1 & (slot1 == slot), w1, 0.0)
        high = full.astype(BF16).astype(F32)
        return jnp.concatenate([high, full - high], axis=0)

    weigh_main = weigh(within).astype(BF16)
    weigh_extra = weigh(TILE + within % EXTRA)
    group = jnp.concatenate([within // EXTRA] * 2, axis=0)

    back_keep.wait()
    for copy in back_copies:
        copy.wait_recv()
    for g in range(GROUPS):
        cols = slice(g * fold, (g + 1) * fold)
        both = jnp.dot(weigh_main, back_v[:, cols], preferred_element_type=F32)
        both += jnp.dot(jnp.where(group == g, weigh_extra, 0.0).astype(BF16), back_v[:, features:], preferred_element_type=F32)
        out_ref[:, cols] = (both[:tok_rows] + both[tok_rows:]).astype(BF16)

    for copy in (out_copies + twin_copies + up_copies + down_copies + on_up + on_down + to_above + to_below
                 + far_below + far_above + back_copies):
        copy.wait_send()


def shards(tokens, expert_ids, route_weights, up_weight, down_weight):
    tok_rows, features = tokens.shape
    units = up_weight.shape[1]
    width = features + features // GROUPS
    vmem = pl.BlockSpec(memory_space=pltpu.VMEM)
    anywhere = pl.BlockSpec(memory_space=pl.ANY)
    dma = pltpu.SemaphoreType.DMA
    return pl.pallas_call(
        kernel,
        out_shape=jax.ShapeDtypeStruct((tok_rows, features), BF16),
        in_specs=[vmem, vmem, vmem, anywhere, anywhere],
        out_specs=vmem,
        scratch_shapes=[
            pltpu.VMEM((2 * units, features), BF16),
            pltpu.VMEM((2 * units, features), BF16),
            pltpu.VMEM((4, ROWS, width), BF16),
            pltpu.VMEM((4, ROWS, width), BF16),
            pltpu.VMEM((PLANE, width), BF16),
            pltpu.VMEM((PLANE, width), BF16),
            pltpu.VMEM((PLANE, width), BF16),
            pltpu.VMEM((PLANE, width), BF16),
            pltpu.VMEM((8 * TILE, width), BF16),
            pltpu.VMEM((ROWS, 2 * units), BF16),
            pltpu.VMEM((PLANE, PLANE), BF16),
            pltpu.VMEM((PLANE, PLANE), BF16),
            dma((2,)), dma((2,)), dma((2,)), dma((2,)),
            dma((PEERS,)), dma((PEERS,)),
            dma((2, PIECES)), dma((2, PIECES)), dma((PIECES,)), dma((PIECES,)),
            dma((PIECES,)), dma((PIECES,)), dma((2, PIECES)), dma((2, PIECES)),
            dma((PEERS,)), dma((PEERS,)),
        ],
        compiler_params=pltpu.CompilerParams(
            collective_id=0, has_side_effects=True, vmem_limit_bytes=63 * 2**20),
        cost_estimate=pl.CostEstimate(
            flops=4 * 4 * ROWS * 2 * units * features, bytes_accessed=6 * units * features, transcendentals=0),
    )(tokens, expert_ids, route_weights, up_weight[0], down_weight[0])


def solution(mesh):
    return jax.shard_map(
        shards,
        mesh=mesh,
        in_specs=(
            P(("expert", "fsdp"), None),
            P(("expert", "fsdp"), None),
            P(("expert", "fsdp"), None),
            P("expert", "fsdp", None),
            P("expert", "fsdp", None),
        ),
        out_specs=P(("expert", "fsdp"), None),
        check_vma=False,
    )
```

time: 335 us -> 151 us (0.45)
  waiting for transfers between devices: 240 us -> 0 us
  Pallas kernels: 0 us -> 146 us
  matrix products: 41 us -> 0 us
  blocking collectives: 22.5 us -> 0 us
  between operations: 13.5 us -> 0.01 us
  other arithmetic: 5.25 us -> 0 us
  starting transfers between devices: 4.36 us -> 0 us
    pallas_call x0 -> x1, Pallas kernels: none -> 146 us  [shards(): pl.pallas_call(kernel, out_shape=jax.ShapeDtypeStruct((tok_rows, features...]
    reduce_scatter x1 -> x0, waiting for transfers between devices: 128 us -> none  [shards(): lax.psum_scatter(jnp.dot(hidden, down_panel, preferred_element_type=jnp.f...]
    all_gather x1 -> x0, waiting for transfers between devices: 97.7 us -> none  [shards(): lax.all_gather(flat_rows, 'fsdp', axis=0, tiled=True)]
    dot_general x3 -> x0, matrix products: 41 us -> none  [the longest x1 20.5 us: shards(): lax.dot_general(lax.all_gather(flat_rows, 'fsdp', axis=0, tiled=True), up...]
    all_to_all x1 -> x0, blocking collectives: 22.5 us -> none  [shards(): lax.all_to_all(outgoing, 'expert', split_axis=0, concat_axis=0, tiled=True)]
    all_to_all x1 -> x0, waiting for transfers between devices: 15.2 us -> none  [shards(): lax.all_to_all(summed.reshape(source_count, slot_count, features), 'exper...]
    unnamed x5 -> x3, local copies, waits for them, and re-layouts: 0.1 us -> 4.52 us
    reduce_sum x3 -> x0, other arithmetic: 4.38 us -> none  [the longest x1 2.93 us: shards(): jnp.sum(route_weights[:, :, None] * picked.astype(jnp.float32), axis=1)]
  transfers between devices with their start and end apart: 3 -> 0, of which waited for: 3 -> 0; matrix products, arithmetic and copies ran while one was open for 0% -> 0% of each run, Pallas kernels for 0% -> 0%
where the time goes in v1:
time: 151 us
  Pallas kernels  146 us (97%)
  local copies, waits for them, and re-layouts  4.52 us (3%)
    pallas_call x1, Pallas kernels, shards(): pl.pallas_call(kernel, out_shape=jax.ShapeDtypeStruct((tok_rows, features...  146 us
    unnamed x3, local copies, waits for them, and re-layouts  4.52 us

profile of v1, /device:TPU:0, one launch (start us, length us, event | category | flops | bytes accessed | tf_op | source)
XLA Modules:
  0.0 150.9 jit_solution(13373809131387048525)
XLA Ops:
  0.0 1.4 copy.6.ids_ref
  1.4 1.4 copy.7.rw_ref
  2.7 146.4 %shard_map.55 = bf16[64,3072]{1,0:T(8,128)(2,1)} custom-call(bf16[64,3072]{1,0:T(8,128)(2,1)} %tok_ref.1, s32[64,2]{1,0:T(8,128)} %copy.6.ids_ref, f32[64,2]{1,0:T(8,128)} %copy.7.rw_ref, bf16[1024,3072]{1,0:T(8,128)(2,1)} %bitcast.2, bf16[1024,3072]{1,0:T(8,128)(2,1)} %bitcast.3), custom_call_target="tpu_custom_call" | custom-call | flops 28991029248 | bytes 18874368 | tf_op jit(solution)/shard_map/pallas_call | solution.py:289
  149.1 1.8 %copy.9 = bf16[64,3072]{1,0:T(8,128)(2,1)} copy(bf16[64,3072]{1,0:T(8,128)(2,1)} %shard_map.55) | data formatting | bytes 786432

commit v2 on v1

v2 whole, which is shorter than its diff:
```python
import jax
import jax.numpy as jnp
from jax import lax
from jax.experimental import pallas as pl
from jax.experimental.pallas import tpu as pltpu
from jax.sharding import PartitionSpec as P

MESH = pl.DeviceIdType.MESH
BF16, F32, I32 = jnp.bfloat16, jnp.float32, jnp.int32

OFFSETS = (
    (0, 0), (1, 1), (3, 3), (2, 2),
    (1, 3), (3, 1), (2, 0), (0, 2),
    (1, 2), (3, 2), (2, 1), (2, 3),
    (1, 0), (3, 0), (0, 1), (0, 3),
)
PEERS = len(OFFSETS)
BLOCKS = 8
TILE = 16
EXTRA = 2
GROUPS = TILE // EXTRA
PIECES = 4
PIECE = PEERS // PIECES * TILE
PLANE = PEERS * TILE
REST = PEERS * EXTRA
ROWS = PLANE + REST
TILE_N = 256
WAY_A, WAY_B = (0, 1), (2, 3)
FIRST_ROWS = (((0,), (0,)), ((), ()))
LAST_COLS = (((1,), (1,)), ((), ()))


def iota(shape, dim):
    return lax.broadcasted_iota(I32, shape, dim)


def onehot(mask):
    return jnp.where(mask, 1.0, 0.0).astype(BF16)


def kernel(
    tok_ref, meta_ref, up_ref, down_ref, out_ref,
    up_v, down_v, xp_v, xz_v, yp_v, yz_v, from_up, from_down, far_v, backp_v, backz_v, sendp_v, sendz_v,
    tok_v, meta_v, part_v, got_v, hid_v, perm_v, permt_v,
    sem_w, sem_ws, sem_wr, sem_self, sem_selfz, sem_ps, sem_pr, sem_as, sem_ar, sem_fs, sem_fr,
    sem_2s, sem_2r, sem_1s, sem_1r, sem_bs, sem_br,
    sem_ts, sem_tr, sem_ms, sem_mr, sem_zs, sem_zr, sem_ys, sem_yr, sem_gs, sem_gr,
):
    tok_rows, features = tok_ref.shape
    units = up_ref.shape[0]
    cols_z = tok_v.shape[2]
    cols_p = features - cols_z
    fold_p, fold_z = cols_p // GROUPS, cols_z // GROUPS
    e, f = lax.axis_index("expert"), lax.axis_index("fsdp")
    x_lo, y = e // 4, e % 4
    z, x_hi, core = f // 4, (f // 2) % 2, f % 2
    x = x_hi * 2 + x_lo

    def device(dx, dy, dz=0, dc=0):
        px, py, pz, pc = (x + dx) % 4, (y + dy) % 4, (z + dz) % 4, (core + dc) % 2
        return {"expert": (px % 2) * 4 + py, "fsdp": (pz * 2 + px // 2) * 2 + pc}

    peers = [device(dx, dy) for dx, dy in OFFSETS]
    backs = [device(-dx, -dy) for dx, dy in OFFSETS]
    planes = [None] + [device(0, 0, j) for j in (1, 2, 3)]
    above, below, twin = planes[1], planes[3], device(0, 0, 0, 1)

    barrier = pltpu.get_barrier_semaphore()
    greeted = peers[1:] + planes[1:] + [twin]
    for other in greeted:
        pl.semaphore_signal(barrier, inc=1, device_id=other, device_id_type=MESH)

    def link(src, dst, send, recv, to):
        return pltpu.make_async_remote_copy(
            src_ref=src, dst_ref=dst, send_sem=send, recv_sem=recv, device_id=to, device_id_type=MESH)

    own_up = pltpu.make_async_copy(up_ref, up_v.at[pl.ds(0, units)], sem_w.at[0])
    own_down = pltpu.make_async_copy(down_ref, down_v.at[pl.ds(0, units)], sem_w.at[1])
    own_up.start()
    own_down.start()

    lane_tok = iota((tok_rows, 2 * tok_rows), 1) % tok_rows
    earlier = onehot(iota((tok_rows, 2 * tok_rows), 0) < lane_tok)

    def slots_of(meta):
        id0, id1 = meta[0:1].astype(I32), meta[1:2].astype(I32)
        rows = iota((TILE, 2 * tok_rows), 0)
        is0, is1 = rows == id0, rows == id1
        chosen = onehot(is0 | is1)[:, :tok_rows]
        before = jnp.dot(chosen, earlier, preferred_element_type=F32)
        slot0 = jnp.sum(jnp.where(is0, before, 0.0), axis=0, keepdims=True).astype(I32)
        slot1 = jnp.sum(jnp.where(is1, before, 0.0), axis=0, keepdims=True).astype(I32)
        return id0, id1, slot0, slot1

    def picks_of(found):
        id0, id1, slot0, slot1 = [v[:, :tok_rows] for v in found]
        place = iota((BLOCKS * TILE, tok_rows), 0)
        block, within = place // TILE, place % TILE
        expert_of = ((x + block // 4) % 2) * 4 + (y + block % 4) % 4
        in0, in1 = id0 == expert_of, id1 == expert_of
        last = TILE + within % EXTRA
        main = onehot((in0 & (slot0 == within)) | (in1 & (slot1 == within)))
        rest = (in0 & (slot0 == last)) | (in1 & (slot1 == last))
        return main, [onehot(rest & (within // EXTRA == g)) for g in range(GROUPS)]

    def fill(dst, picks, src, first, cols):
        main, rest = picks
        fold = cols // GROUPS
        dst[:, 0:cols] = jnp.dot(main, src[:, first:first + cols], preferred_element_type=F32).astype(BF16)
        extra = jnp.zeros((BLOCKS * TILE, fold), F32)
        for g in range(GROUPS):
            extra += jnp.dot(rest[g], src[:, first + g * fold:first + (g + 1) * fold], preferred_element_type=F32)
        dst[:, cols:cols + fold] = extra.astype(BF16)

    own_slots = slots_of(meta_ref[...])
    own_picks = picks_of(own_slots)
    fill(sendp_v, own_picks, tok_ref, 0, cols_p)

    pl.semaphore_wait(barrier, len(greeted))

    tok_copies = [None] + [
        link(tok_ref.at[:, pl.ds(cols_p, cols_z)], tok_v.at[4 - j], sem_ts.at[j], sem_tr.at[4 - j], planes[j]) for j in (1, 2, 3)]
    meta_copies = [None] + [
        link(meta_ref, meta_v.at[4 - j], sem_ms.at[j], sem_mr.at[4 - j], planes[j]) for j in (1, 2, 3)]
    for j in (1, 3, 2):
        meta_copies[j].start()
        tok_copies[j].start()

    def from_block(r):
        dx, dy = OFFSETS[r]
        return pl.ds(((dx % 2) * 4 + dy) * TILE, TILE)

    def at_block(r):
        return pl.ds(r * TILE, TILE)

    keep = pltpu.make_async_copy(sendp_v.at[from_block(0)], xp_v.at[0, at_block(0)], sem_self.at[0])
    keep.start()
    out_copies = [
        link(sendp_v.at[from_block(r)], xp_v.at[0, at_block(r)], sem_ps.at[r], sem_pr.at[r], peers[r]) for r in range(1, PEERS)]
    for copy in out_copies:
        copy.start()

    keep_z = [pltpu.make_async_copy(sendz_v.at[j, from_block(0)], xz_v.at[j, at_block(0)], sem_selfz.at[0, j]) for j in range(4)]
    out_z = [
        [link(sendz_v.at[j, from_block(r)], xz_v.at[j, at_block(r)], sem_zs.at[j, r], sem_zr.at[j, r], peers[r])
         for r in range(1, PEERS)] for j in range(4)]

    def spread_z(j, picks, src, first):
        fill(sendz_v.at[j], picks, src, first, cols_z)
        keep_z[j].start()
        for copy in out_z[j]:
            copy.start()

    spread_z(0, own_picks, tok_ref, cols_p)

    twin_copies = [
        link(src, dst.at[pl.ds(units, units)], sem_ws.at[i], sem_wr.at[i], twin)
        for i, (src, dst) in enumerate(((up_ref, up_v), (down_ref, down_v)))]
    for copy in twin_copies:
        copy.start()

    out_row, in_row = iota((PLANE, PLANE), 0), iota((PLANE, PLANE), 1)
    perm_v[...] = onehot(in_row == (out_row % REST) // EXTRA * TILE + out_row // REST * EXTRA + out_row % EXTRA)
    permt_v[...] = onehot(out_row == (in_row % REST) // EXTRA * TILE + in_row // REST * EXTRA + in_row % EXTRA)

    def piece(k):
        return pl.ds(k * PIECE, PIECE)

    up_copies = [link(xp_v.at[0, piece(k)], xp_v.at[3, piece(k)], sem_as.at[0, k], sem_ar.at[0, k], above) for k in range(PIECES)]
    down_copies = [link(xp_v.at[0, piece(k)], xp_v.at[1, piece(k)], sem_as.at[1, k], sem_ar.at[1, k], below) for k in range(PIECES)]
    on_up = [link(xp_v.at[3, piece(k)], xp_v.at[2, piece(k)], sem_fs.at[k], sem_fr.at[k], above) for k in WAY_A]
    on_down = [link(xp_v.at[1, piece(k)], xp_v.at[2, piece(k)], sem_fs.at[k], sem_fr.at[k], below) for k in WAY_B]

    slots = [own_slots, None, None, None]
    for k in range(PIECES):
        for r in range(k * PEERS // PIECES, (k + 1) * PEERS // PIECES):
            if r == 0:
                keep.wait()
            else:
                out_copies[r - 1].wait_recv()
        up_copies[k].start()
        down_copies[k].start()
        if k < 3:
            j = (1, 3, 2)[k]
            meta_copies[4 - j].wait_recv()
            tok_copies[4 - j].wait_recv()
            slots[j] = slots_of(meta_v[j])
            spread_z(j, picks_of(slots[j]), tok_v.at[j], 0)

    parts = ((xp_v, yp_v, fold_p, cols_p), (xz_v, yz_v, fold_z, cols_z))

    def unfold(j):
        for x_v, _, fold, cols in parts:
            moved = jnp.dot(perm_v[...], x_v[j, 0:PLANE, cols:], preferred_element_type=F32).astype(BF16)
            for g in range(GROUPS):
                x_v[j, PLANE:ROWS, g * fold:(g + 1) * fold] = moved[g * REST:(g + 1) * REST]

    def refold(j, part):
        _, y_v, fold, cols = parts[part]
        total = jnp.zeros((PLANE, fold), F32)
        for g in range(GROUPS):
            total += jnp.dot(permt_v[:, g * REST:(g + 1) * REST], y_v[j, PLANE:ROWS, g * fold:(g + 1) * fold],
                             preferred_element_type=F32)
        y_v[j, 0:PLANE, cols:] = total.astype(BF16)

    def into_hidden(j, first, count):
        def body(n, carry):
            at = pl.ds(pl.multiple_of(n * TILE_N, TILE_N), TILE_N)
            v = lax.dot_general(xp_v[j, :, :cols_p], up_v[at, :cols_p], LAST_COLS, preferred_element_type=F32)
            v += lax.dot_general(xz_v[j, :, :cols_z], up_v[at, cols_p:], LAST_COLS, preferred_element_type=F32)
            hid_v[:, at] = (v / (1.0 + jnp.exp(-v))).astype(BF16)
            return carry

        lax.fori_loop(first // TILE_N, (first + count) // TILE_N, body, 0)

    def out_of_hidden(j, part):
        _, y_v, _, cols = parts[part]
        start = part * cols_p

        def body(n, carry):
            at = pl.ds(pl.multiple_of(n * TILE_N, TILE_N), TILE_N)
            down_at = pl.ds(pl.multiple_of(start + n * TILE_N, TILE_N), TILE_N)
            y_v[j, :, at] = jnp.dot(hid_v[...], down_v[:, down_at], preferred_element_type=F32).astype(BF16)
            return carry

        lax.fori_loop(0, cols // TILE_N, body, 0)
        refold(j, part)

    backz_keep = [pltpu.make_async_copy(yz_v.at[j, at_block(0)], backz_v.at[j, at_block(0)], sem_selfz.at[1, j]) for j in range(4)]
    backz_copies = [
        [link(yz_v.at[j, at_block(r)], backz_v.at[j, at_block(r)], sem_ys.at[j, r], sem_yr.at[j, r], backs[r])
         for r in range(1, PEERS)] for j in range(4)]

    def return_z(j):
        out_of_hidden(j, 1)
        backz_keep[j].start()
        for copy in backz_copies[j]:
            copy.start()

    def arrive_z(j):
        keep_z[j].wait()
        for copy in out_z[j]:
            copy.wait_recv()

    arrive_z(0)
    unfold(0)
    own_up.wait()
    into_hidden(0, 0, units)
    twin_copies[0].wait_recv()
    into_hidden(0, units, units)
    own_down.wait()
    twin_copies[1].wait_recv()
    return_z(0)
    out_of_hidden(0, 0)

    for i in range(len(WAY_A)):
        up_copies[WAY_A[i]].wait_recv()
        on_up[i].start()
    for k in range(PIECES):
        down_copies[k].wait_recv()
        if k in WAY_B:
            on_down[WAY_B.index(k)].start()
    for k in WAY_B:
        up_copies[k].wait_recv()

    to_above = [link(yp_v.at[1, piece(k)], from_down.at[piece(k)], sem_1s.at[0, k], sem_1r.at[0, k], above) for k in range(PIECES)]
    to_below = [link(yp_v.at[3, piece(k)], from_up.at[piece(k)], sem_1s.at[1, k], sem_1r.at[1, k], below) for k in range(PIECES)]
    far_below = [link(yp_v.at[2, piece(k)], far_v.at[piece(k)], sem_2s.at[k], sem_2r.at[k], below) for k in WAY_A]
    far_above = [link(yp_v.at[2, piece(k)], far_v.at[piece(k)], sem_2s.at[k], sem_2r.at[k], above) for k in WAY_B]

    def enter(j):
        arrive_z(j)
        unfold(j)
        into_hidden(j, 0, 2 * units)
        out_of_hidden(j, 0)

    enter(1)
    for k in WAY_A:
        to_above[k].start()
    return_z(1)
    enter(3)
    for k in WAY_B:
        to_below[k].start()
    return_z(3)
    for copy in on_up + on_down:
        copy.wait_recv()
    enter(2)
    for copy in far_below + far_above:
        copy.start()
    return_z(2)

    place = iota((PLANE, 2 * tok_rows), 0)
    block, within = place // TILE, place % TILE
    dx, dy = jnp.zeros_like(place), jnp.zeros_like(place)
    for r, (rx, ry) in enumerate(OFFSETS):
        dx, dy = jnp.where(block == r, rx, dx), jnp.where(block == r, ry, dy)
    expert_of = ((x + dx) % 2) * 4 + (y + dy) % 4
    is_high = iota((PLANE, 2 * tok_rows), 1) < tok_rows

    def weigh(found, meta, slot):
        id0, id1, slot0, slot1 = found
        full = (jnp.where((id0 == expert_of) & (slot0 == slot), meta[2:3], 0.0)
                + jnp.where((id1 == expert_of) & (slot1 == slot), meta[3:4], 0.0))
        high = full.astype(BF16).astype(F32)
        return jnp.where(is_high, high, full - high)

    def combine(found, meta, src, cols, put):
        fold = cols // GROUPS
        main = weigh(found, meta, within).astype(BF16)
        rest = weigh(found, meta, TILE + within % EXTRA)
        for g in range(GROUPS):
            at = slice(g * fold, (g + 1) * fold)
            both = lax.dot_general(main, src[:, at], FIRST_ROWS, preferred_element_type=F32)
            both += lax.dot_general(jnp.where(within // EXTRA == g, rest, 0.0).astype(BF16), src[:, cols:],
                                    FIRST_ROWS, preferred_element_type=F32)
            put(at, both[:tok_rows] + both[tok_rows:])

    part_copies = [None] + [link(part_v.at[j], got_v.at[j], sem_gs.at[j], sem_gr.at[j], planes[j]) for j in (1, 2, 3)]

    def gather_z(j):
        backz_keep[j].wait()
        for copy in backz_copies[j]:
            copy.wait_recv()

        def put(at, value):
            part_v[j, :, at] = value.astype(BF16)

        combine(slots[j], meta_ref[...] if j == 0 else meta_v[j], backz_v.at[j], cols_z, put)
        if j:
            part_copies[j].start()

    gather_z(0)
    gather_z(1)

    def add_into(target, j, k, others):
        total = target[j, piece(k), :].astype(F32)
        for other in others:
            total += other[piece(k), :].astype(F32)
        target[j, piece(k), :] = total.astype(BF16)

    for i in range(len(WAY_A)):
        far_below[i].wait_recv()
        add_into(yp_v, 3, WAY_A[i], (far_v,))
        to_below[WAY_A[i]].start()
        far_above[i].wait_recv()
        add_into(yp_v, 1, WAY_B[i], (far_v,))
        to_above[WAY_B[i]].start()

    gather_z(3)
    gather_z(2)

    back_keep = pltpu.make_async_copy(yp_v.at[0, at_block(0)], backp_v.at[at_block(0)], sem_self.at[1])
    back_copies = [
        link(yp_v.at[0, at_block(r)], backp_v.at[at_block(r)], sem_bs.at[r], sem_br.at[r], backs[r]) for r in range(1, PEERS)]
    for k in (0, 2, 1, 3):
        to_above[k].wait_recv()
        to_below[k].wait_recv()
        add_into(yp_v, 0, k, (from_up, from_down))
        for r in range(k * PEERS // PIECES, (k + 1) * PEERS // PIECES):
            (back_keep if r == 0 else back_copies[r - 1]).start()

    for j in (1, 2, 3):
        part_copies[j].wait_recv()
    total = part_v[0].astype(F32)
    for j in (1, 2, 3):
        total += got_v[j].astype(F32)
    out_ref[:, cols_p:] = total.astype(BF16)

    back_keep.wait()
    for copy in back_copies:
        copy.wait_recv()

    def put_out(at, value):
        out_ref[:, at] = value.astype(BF16)

    combine(own_slots, meta_ref[...], backp_v, cols_p, put_out)

    for copy in (out_copies + twin_copies + up_copies + down_copies + on_up + on_down + to_above + to_below
                 + far_below + far_above + back_copies + tok_copies[1:] + meta_copies[1:] + part_copies[1:]):
        copy.wait_send()
    for j in range(4):
        for copy in out_z[j] + backz_copies[j]:
            copy.wait_send()


def shards(tokens, expert_ids, route_weights, up_weight, down_weight):
    tok_rows, features = tokens.shape
    units = up_weight.shape[1]
    cols_z = features // 3
    cols_p = features - cols_z
    wide_p, wide_z = cols_p + cols_p // GROUPS, cols_z + cols_z // GROUPS
    meta = jnp.concatenate([expert_ids.T.astype(F32), route_weights.T, jnp.zeros((4, tok_rows), F32)], axis=0)
    meta = jnp.concatenate([meta, meta], axis=1)
    vmem = pl.BlockSpec(memory_space=pltpu.VMEM)
    anywhere = pl.BlockSpec(memory_space=pl.ANY)
    dma = pltpu.SemaphoreType.DMA
    return pl.pallas_call(
        kernel,
        out_shape=jax.ShapeDtypeStruct((tok_rows, features), BF16),
        in_specs=[vmem, vmem, anywhere, anywhere],
        out_specs=vmem,
        scratch_shapes=[
            pltpu.VMEM((2 * units, features), BF16),
            pltpu.VMEM((2 * units, features), BF16),
            pltpu.VMEM((4, ROWS, wide_p), BF16),
            pltpu.VMEM((4, ROWS, wide_z), BF16),
            pltpu.VMEM((4, ROWS, wide_p), BF16),
            pltpu.VMEM((4, ROWS, wide_z), BF16),
            pltpu.VMEM((PLANE, wide_p), BF16),
            pltpu.VMEM((PLANE, wide_p), BF16),
            pltpu.VMEM((PLANE, wide_p), BF16),
            pltpu.VMEM((PLANE, wide_p), BF16),
            pltpu.VMEM((4, PLANE, wide_z), BF16),
            pltpu.VMEM((BLOCKS * TILE, wide_p), BF16),
            pltpu.VMEM((4, BLOCKS * TILE, wide_z), BF16),
            pltpu.VMEM((4, tok_rows, cols_z), BF16),
            pltpu.VMEM((4, 8, 2 * tok_rows), F32),
            pltpu.VMEM((4, tok_rows, cols_z), BF16),
            pltpu.VMEM((4, tok_rows, cols_z), BF16),
            pltpu.VMEM((ROWS, 2 * units), BF16),
            pltpu.VMEM((PLANE, PLANE), BF16),
            pltpu.VMEM((PLANE, PLANE), BF16),
            dma((2,)), dma((2,)), dma((2,)), dma((2,)), dma((2, 4)),
            dma((PEERS,)), dma((PEERS,)),
            dma((2, PIECES)), dma((2, PIECES)), dma((PIECES,)), dma((PIECES,)),
            dma((PIECES,)), dma((PIECES,)), dma((2, PIECES)), dma((2, PIECES)),
            dma((PEERS,)), dma((PEERS,)),
            dma((4,)), dma((4,)), dma((4,)), dma((4,)),
            dma((4, PEERS)), dma((4, PEERS)), dma((4, PEERS)), dma((4, PEERS)), dma((4,)), dma((4,)),
        ],
        compiler_params=pltpu.CompilerParams(
            collective_id=0, has_side_effects=True, vmem_limit_bytes=63 * 2**20),
        cost_estimate=pl.CostEstimate(
            flops=4 * 4 * ROWS * 2 * units * features, bytes_accessed=6 * units * features, transcendentals=0),
    )(tokens, meta, up_weight[0], down_weight[0])


def solution(mesh):
    return jax.shard_map(
        shards,
        mesh=mesh,
        in_specs=(
            P(("expert", "fsdp"), None),
            P(("expert", "fsdp"), None),
            P(("expert", "fsdp"), None),
            P("expert", "fsdp", None),
            P("expert", "fsdp", None),
        ),
        out_specs=P(("expert", "fsdp"), None),
        check_vma=False,
    )
```

time: 151 us -> 125 us (0.83)
  Pallas kernels: 146 us -> 121 us
  local copies, waits for them, and re-layouts: 4.52 us -> 1.77 us
  other arithmetic: 0 us -> 2.1 us
    pallas_call x1, Pallas kernels: 146 us -> 121 us  [shards(): pl.pallas_call(kernel, out_shape=jax.ShapeDtypeStruct((tok_rows, features...]
    unnamed x3 -> x1, local copies, waits for them, and re-layouts: 4.52 us -> 1.77 us
where the time goes in v2:
time: 125 us
  Pallas kernels  121 us (97%)
  other arithmetic  2.1 us (2%)
  local copies, waits for them, and re-layouts  1.77 us (1%)
    pallas_call x1, Pallas kernels, shards(): pl.pallas_call(kernel, out_shape=jax.ShapeDtypeStruct((tok_rows, features...  121 us

profile of v2, /device:TPU:0, one launch (start us, length us, event | category | flops | bytes accessed | tf_op | source)
XLA Modules:
  0.0 125.2 jit_solution(8634011835241967964)
XLA Ops:
  0.0 0.7 convert_bitcast_fusion
  0.7 1.4 %maximum_maximum_fusion.meta_ref = f32[8,128]{1,0:T(8,128)} fusion(f32[4,64]{1,0:T(4,128)S(1)} %broadcast_in_dim.3, f32[2,64]{1,0:T(2,128)} %bitcast.5, f32[2,64]{1,0:T(2,128)S(1)} %convert_bitcast_fusion), kind=kLoop, calls=%fused_computation | loop fusion | flops 5120 | bytes 6144 | tf_op jit(solution)/shard_map/concatenate | solution.py:393
  2.1 121.3 %shard_map.55 = bf16[64,3072]{1,0:T(8,128)(2,1)} custom-call(bf16[64,3072]{1,0:T(8,128)(2,1)} %tok_ref.1, f32[8,128]{1,0:T(8,128)} %maximum_maximum_fusion.meta_ref, bf16[1024,3072]{1,0:T(8,128)(2,1)} %bitcast.6, bf16[1024,3072]{1,0:T(8,128)(2,1)} %bitcast.7), custom_call_target="tpu_custom_call" | custom-call | flops 28991029248 | bytes 18874368 | tf_op jit(solution)/shard_map/pallas_call | solution.py:397
  123.4 1.8 %copy.7 = bf16[64,3072]{1,0:T(8,128)(2,1)} copy(bf16[64,3072]{1,0:T(8,128)(2,1)} %shard_map.55) | data formatting | bytes 786432
  (1 shorter events, 0.0 us)

commit v3 on v2

--- a/solution.py
+++ b/solution.py
@@ -10,10 +10,11 @@
 
 OFFSETS = (
     (0, 0), (1, 1), (3, 3), (2, 2),
+    (1, 2), (3, 2), (2, 1), (2, 3),
     (1, 3), (3, 1), (2, 0), (0, 2),
-    (1, 2), (3, 2), (2, 1), (2, 3),
     (1, 0), (3, 0), (0, 1), (0, 3),
 )
+PIECE_ORDER = (0, 2, 1, 3)
 PEERS = len(OFFSETS)
 BLOCKS = 8
 TILE = 16
@@ -24,12 +25,24 @@
 PLANE = PEERS * TILE
 REST = PEERS * EXTRA
 ROWS = PLANE + REST
-TILE_N = 256
+TILE_N = 1024
 WAY_A, WAY_B = (0, 1), (2, 3)
 FIRST_ROWS = (((0,), (0,)), ((), ()))
 LAST_COLS = (((1,), (1,)), ((), ()))
 
 
+def batch_of(j, k):
+    return j if j % 2 == 0 or k in WAY_A else 4 - j
+
+
+def pairs_of(batch):
+    return [(j, k) for j in range(4) for k in range(PIECES) if batch_of(j, k) == batch]
+
+
+def offsets_of(k):
+    return range(k * PEERS // PIECES, (k + 1) * PEERS // PIECES)
+
+
 def iota(shape, dim):
     return lax.broadcasted_iota(I32, shape, dim)
 
@@ -39,7 +52,7 @@
 
 
 def kernel(
-    tok_ref, meta_ref, up_ref, down_ref, out_ref,
+    tok_ref, ids_ref, rw_ref, up_ref, down_ref, out_ref,
     up_v, down_v, xp_v, xz_v, yp_v, yz_v, from_up, from_down, far_v, backp_v, backz_v, sendp_v, sendz_v,
     tok_v, meta_v, part_v, got_v, hid_v, perm_v, permt_v,
     sem_w, sem_ws, sem_wr, sem_self, sem_selfz, sem_ps, sem_pr, sem_as, sem_ar, sem_fs, sem_fr,
@@ -112,6 +125,11 @@
             extra += jnp.dot(rest[g], src[:, first + g * fold:first + (g + 1) * fold], preferred_element_type=F32)
         dst[:, cols:cols + fold] = extra.astype(BF16)
 
+    meta_ref = meta_v.at[0]
+    meta_v[0] = jnp.zeros((8, 2 * tok_rows), F32)
+    for at in (slice(0, tok_rows), slice(tok_rows, 2 * tok_rows)):
+        meta_v[0, 0:2, at] = ids_ref[...].astype(F32)
+        meta_v[0, 2:4, at] = rw_ref[...]
     own_slots = slots_of(meta_ref[...])
     own_picks = picks_of(own_slots)
     fill(sendp_v, own_picks, tok_ref, 0, cols_p)
@@ -137,21 +155,21 @@
     keep.start()
     out_copies = [
         link(sendp_v.at[from_block(r)], xp_v.at[0, at_block(r)], sem_ps.at[r], sem_pr.at[r], peers[r]) for r in range(1, PEERS)]
-    for copy in out_copies:
-        copy.start()
-
-    keep_z = [pltpu.make_async_copy(sendz_v.at[j, from_block(0)], xz_v.at[j, at_block(0)], sem_selfz.at[0, j]) for j in range(4)]
+    for k in PIECE_ORDER:
+        for r in offsets_of(k):
+            if r:
+                out_copies[r - 1].start()
+
+    keep_z = [pltpu.make_async_copy(sendz_v.at[j, from_block(0)], xz_v.at[batch_of(j, 0), at_block(0)], sem_selfz.at[0, j]) for j in range(4)]
     out_z = [
-        [link(sendz_v.at[j, from_block(r)], xz_v.at[j, at_block(r)], sem_zs.at[j, r], sem_zr.at[j, r], peers[r])
+        [link(sendz_v.at[j, from_block(r)], xz_v.at[batch_of(j, r * PIECES // PEERS), at_block(r)], sem_zs.at[j, r], sem_zr.at[j, r], peers[r])
          for r in range(1, PEERS)] for j in range(4)]
 
     def spread_z(j, picks, src, first):
         fill(sendz_v.at[j], picks, src, first, cols_z)
-        keep_z[j].start()
-        for copy in out_z[j]:
-            copy.start()
-
-    spread_z(0, own_picks, tok_ref, cols_p)
+        for k in PIECE_ORDER:
+            for r in offsets_of(k):
+                (out_z[j][r - 1] if r else keep_z[j]).start()
 
     twin_copies = [
         link(src, dst.at[pl.ds(units, units)], sem_ws.at[i], sem_wr.at[i], twin)
@@ -166,26 +184,35 @@
     def piece(k):
         return pl.ds(k * PIECE, PIECE)
 
-    up_copies = [link(xp_v.at[0, piece(k)], xp_v.at[3, piece(k)], sem_as.at[0, k], sem_ar.at[0, k], above) for k in range(PIECES)]
-    down_copies = [link(xp_v.at[0, piece(k)], xp_v.at[1, piece(k)], sem_as.at[1, k], sem_ar.at[1, k], below) for k in range(PIECES)]
-    on_up = [link(xp_v.at[3, piece(k)], xp_v.at[2, piece(k)], sem_fs.at[k], sem_fr.at[k], above) for k in WAY_A]
-    on_down = [link(xp_v.at[1, piece(k)], xp_v.at[2, piece(k)], sem_fs.at[k], sem_fr.at[k], below) for k in WAY_B]
+    def xp_at(j, k):
+        return xp_v.at[batch_of(j, k), piece(k)]
+
+    def yp_at(j, k):
+        return yp_v.at[batch_of(j, k), piece(k)]
+
+    up_copies = [link(xp_at(0, k), xp_at(3, k), sem_as.at[0, k], sem_ar.at[0, k], above) for k in range(PIECES)]
+    down_copies = [link(xp_at(0, k), xp_at(1, k), sem_as.at[1, k], sem_ar.at[1, k], below) for k in range(PIECES)]
+    on_down = {k: link(xp_at(1, k), xp_at(2, k), sem_fs.at[k], sem_fr.at[k], below) for k in WAY_A}
+    on_up = {k: link(xp_at(3, k), xp_at(2, k), sem_fs.at[k], sem_fr.at[k], above) for k in WAY_B}
 
     slots = [own_slots, None, None, None]
-    for k in range(PIECES):
-        for r in range(k * PEERS // PIECES, (k + 1) * PEERS // PIECES):
+    for k, j in zip(PIECE_ORDER, (1, 3, 0, 2)):
+        if j:
+            meta_copies[4 - j].wait_recv()
+            tok_copies[4 - j].wait_recv()
+            slots[j] = slots_of(meta_v[j])
+            spread_z(j, picks_of(slots[j]), tok_v.at[j], 0)
+        else:
+            spread_z(0, own_picks, tok_ref, cols_p)
+        for r in offsets_of(k):
             if r == 0:
                 keep.wait()
             else:
                 out_copies[r - 1].wait_recv()
-        up_copies[k].start()
-        down_copies[k].start()
-        if k < 3:
-            j = (1, 3, 2)[k]
-            meta_copies[4 - j].wait_recv()
-            tok_copies[4 - j].wait_recv()
-            slots[j] = slots_of(meta_v[j])
-            spread_z(j, picks_of(slots[j]), tok_v.at[j], 0)
+        (down_copies if k in WAY_A else up_copies)[k].start()
+    for a, b in zip(WAY_A, WAY_B):
+        down_copies[b].start()
+        up_copies[a].start()
 
     parts = ((xp_v, yp_v, fold_p, cols_p), (xz_v, yz_v, fold_z, cols_z))
 
@@ -203,7 +230,7 @@
                              preferred_element_type=F32)
         y_v[j, 0:PLANE, cols:] = total.astype(BF16)
 
-    def into_hidden(j, first, count):
+    def into_hidden(j):
         def body(n, carry):
             at = pl.ds(pl.multiple_of(n * TILE_N, TILE_N), TILE_N)
             v = lax.dot_general(xp_v[j, :, :cols_p], up_v[at, :cols_p], LAST_COLS, preferred_element_type=F32)
@@ -211,7 +238,7 @@
             hid_v[:, at] = (v / (1.0 + jnp.exp(-v))).astype(BF16)
             return carry
 
-        lax.fori_loop(first // TILE_N, (first + count) // TILE_N, body, 0)
+        lax.fori_loop(0, 2 * units // TILE_N, body, 0)
 
     def out_of_hidden(j, part):
         _, y_v, _, cols = parts[part]
@@ -226,67 +253,59 @@
         lax.fori_loop(0, cols // TILE_N, body, 0)
         refold(j, part)
 
-    backz_keep = [pltpu.make_async_copy(yz_v.at[j, at_block(0)], backz_v.at[j, at_block(0)], sem_selfz.at[1, j]) for j in range(4)]
+    backz_keep = [pltpu.make_async_copy(yz_v.at[batch_of(j, 0), at_block(0)], backz_v.at[j, at_block(0)], sem_selfz.at[1, j]) for j in range(4)]
     backz_copies = [
-        [link(yz_v.at[j, at_block(r)], backz_v.at[j, at_block(r)], sem_ys.at[j, r], sem_yr.at[j, r], backs[r])
+        [link(yz_v.at[batch_of(j, r * PIECES // PEERS), at_block(r)], backz_v.at[j, at_block(r)], sem_ys.at[j, r], sem_yr.at[j, r], backs[r])
          for r in range(1, PEERS)] for j in range(4)]
 
-    def return_z(j):
-        out_of_hidden(j, 1)
-        backz_keep[j].start()
-        for copy in backz_copies[j]:
-            copy.start()
-
-    def arrive_z(j):
-        keep_z[j].wait()
-        for copy in out_z[j]:
-            copy.wait_recv()
-
-    arrive_z(0)
-    unfold(0)
+    def return_z(batch):
+        out_of_hidden(batch, 1)
+        for j, k in pairs_of(batch):
+            for r in offsets_of(k):
+                (backz_copies[j][r - 1] if r else backz_keep[j]).start()
+
+    def enter(batch):
+        for j, k in pairs_of(batch):
+            for r in offsets_of(k):
+                if r:
+                    out_z[j][r - 1].wait_recv()
+                else:
+                    keep_z[j].wait()
+        unfold(batch)
+        into_hidden(batch)
+        out_of_hidden(batch, 0)
+
+    to_above = [link(yp_at(1, k), from_down.at[piece(k)], sem_1s.at[0, k], sem_1r.at[0, k], above) for k in range(PIECES)]
+    to_below = [link(yp_at(3, k), from_up.at[piece(k)], sem_1s.at[1, k], sem_1r.at[1, k], below) for k in range(PIECES)]
+    far_below = {k: link(yp_at(2, k), far_v.at[piece(k)], sem_2s.at[k], sem_2r.at[k], below) for k in WAY_A}
+    far_above = {k: link(yp_at(2, k), far_v.at[piece(k)], sem_2s.at[k], sem_2r.at[k], above) for k in WAY_B}
+
+    for a, b in zip(WAY_A, WAY_B):
+        down_copies[a].wait_recv()
+        on_down[a].start()
+        up_copies[b].wait_recv()
+        on_up[b].start()
     own_up.wait()
-    into_hidden(0, 0, units)
     twin_copies[0].wait_recv()
-    into_hidden(0, units, units)
     own_down.wait()
     twin_copies[1].wait_recv()
-    return_z(0)
-    out_of_hidden(0, 0)
-
-    for i in range(len(WAY_A)):
-        up_copies[WAY_A[i]].wait_recv()
-        on_up[i].start()
-    for k in range(PIECES):
-        down_copies[k].wait_recv()
-        if k in WAY_B:
-            on_down[WAY_B.index(k)].start()
-    for k in WAY_B:
-        up_copies[k].wait_recv()
-
-    to_above = [link(yp_v.at[1, piece(k)], from_down.at[piece(k)], sem_1s.at[0, k], sem_1r.at[0, k], above) for k in range(PIECES)]
-    to_below = [link(yp_v.at[3, piece(k)], from_up.at[piece(k)], sem_1s.at[1, k], sem_1r.at[1, k], below) for k in range(PIECES)]
-    far_below = [link(yp_v.at[2, piece(k)], far_v.at[piece(k)], sem_2s.at[k], sem_2r.at[k], below) for k in WAY_A]
-    far_above = [link(yp_v.at[2, piece(k)], far_v.at[piece(k)], sem_2s.at[k], sem_2r.at[k], above) for k in WAY_B]
-
-    def enter(j):
-        arrive_z(j)
-        unfold(j)
-        into_hidden(j, 0, 2 * units)
-        out_of_hidden(j, 0)
-
     enter(1)
-    for k in WAY_A:
-        to_above[k].start()
+    for a, b in zip(WAY_A, WAY_B):
+        to_above[a].start()
+        to_below[b].start()
     return_z(1)
+    for a, b in zip(WAY_A, WAY_B):
+        down_copies[b].wait_recv()
+        up_copies[a].wait_recv()
     enter(3)
-    for k in WAY_B:
-        to_below[k].start()
     return_z(3)
-    for copy in on_up + on_down:
-        copy.wait_recv()
+    for a, b in zip(WAY_A, WAY_B):
+        on_down[a].wait_recv()
+        on_up[b].wait_recv()
     enter(2)
-    for copy in far_below + far_above:
-        copy.start()
+    for a, b in zip(WAY_A, WAY_B):
+        far_below[a].start()
+        far_above[b].start()
     return_z(2)
 
     place = iota((PLANE, 2 * tok_rows), 0)
@@ -329,8 +348,9 @@
         if j:
             part_copies[j].start()
 
-    gather_z(0)
     gather_z(1)
+    enter(0)
+    return_z(0)
 
     def add_into(target, j, k, others):
         total = target[j, piece(k), :].astype(F32)
@@ -338,25 +358,24 @@
             total += other[piece(k), :].astype(F32)
         target[j, piece(k), :] = total.astype(BF16)
 
-    for i in range(len(WAY_A)):
-        far_below[i].wait_recv()
-        add_into(yp_v, 3, WAY_A[i], (far_v,))
-        to_below[WAY_A[i]].start()
-        far_above[i].wait_recv()
-        add_into(yp_v, 1, WAY_B[i], (far_v,))
-        to_above[WAY_B[i]].start()
-
-    gather_z(3)
-    gather_z(2)
+    for a, b, j in zip(WAY_A, WAY_B, (3, 2)):
+        far_below[a].wait_recv()
+        add_into(yp_v, 3, a, (far_v,))
+        to_below[a].start()
+        far_above[b].wait_recv()
+        add_into(yp_v, 3, b, (far_v,))
+        to_above[b].start()
+        gather_z(j)
+    gather_z(0)
 
     back_keep = pltpu.make_async_copy(yp_v.at[0, at_block(0)], backp_v.at[at_block(0)], sem_self.at[1])
     back_copies = [
         link(yp_v.at[0, at_block(r)], backp_v.at[at_block(r)], sem_bs.at[r], sem_br.at[r], backs[r]) for r in range(1, PEERS)]
-    for k in (0, 2, 1, 3):
+    for k in PIECE_ORDER:
         to_above[k].wait_recv()
         to_below[k].wait_recv()
         add_into(yp_v, 0, k, (from_up, from_down))
-        for r in range(k * PEERS // PIECES, (k + 1) * PEERS // PIECES):
+        for r in offsets_of(k):
             (back_keep if r == 0 else back_copies[r - 1]).start()
 
     for j in (1, 2, 3):
@@ -375,8 +394,8 @@
 
     combine(own_slots, meta_ref[...], backp_v, cols_p, put_out)
 
-    for copy in (out_copies + twin_copies + up_copies + down_copies + on_up + on_down + to_above + to_below
-                 + far_below + far_above + back_copies + tok_copies[1:] + meta_copies[1:] + part_copies[1:]):
+    onward = [way[k] for way in (on_up, on_down, far_below, far_above) for k in sorted(way)]
+    for copy in (out_copies + twin_copies + up_copies + down_copies + to_above + to_below + onward + back_copies + tok_copies[1:] + meta_copies[1:] + part_copies[1:]):
         copy.wait_send()
     for j in range(4):
         for copy in out_z[j] + backz_copies[j]:
@@ -389,15 +408,13 @@
     cols_z = features // 3
     cols_p = features - cols_z
     wide_p, wide_z = cols_p + cols_p // GROUPS, cols_z + cols_z // GROUPS
-    meta = jnp.concatenate([expert_ids.T.astype(F32), route_weights.T, jnp.zeros((4, tok_rows), F32)], axis=0)
-    meta = jnp.concatenate([meta, meta], axis=1)
     vmem = pl.BlockSpec(memory_space=pltpu.VMEM)
     anywhere = pl.BlockSpec(memory_space=pl.ANY)
     dma = pltpu.SemaphoreType.DMA
     return pl.pallas_call(
         kernel,
         out_shape=jax.ShapeDtypeStruct((tok_rows, features), BF16),
-        in_specs=[vmem, vmem, anywhere, anywhere],
+        in_specs=[vmem, vmem, vmem, anywhere, anywhere],
         out_specs=vmem,
         scratch_shapes=[
             pltpu.VMEM((2 * units, features), BF16),
@@ -432,7 +449,7 @@
             collective_id=0, has_side_effects=True, vmem_limit_bytes=63 * 2**20),
         cost_estimate=pl.CostEstimate(
             flops=4 * 4 * ROWS * 2 * units * features, bytes_accessed=6 * units * features, transcendentals=0),
-    )(tokens, meta, up_weight[0], down_weight[0])
+    )(tokens, expert_ids.T, route_weights.T, up_weight[0], down_weight[0])
 
 
 def solution(mesh):

time: 125 us -> 115 us (0.920)
  Pallas kernels: 121 us -> 113 us
  other arithmetic: 2.1 us -> 0 us
    pallas_call x1, Pallas kernels: 121 us -> 113 us  [shards(): pl.pallas_call(kernel, out_shape=jax.ShapeDtypeStruct((tok_rows, features...]
    concatenate x1 -> x0, other arithmetic: 1.42 us -> none  [shards(): meta = jnp.concatenate([meta, meta], axis=1)]
where the time goes in v3:
time: 115 us
  Pallas kernels  113 us (98%)
  local copies, waits for them, and re-layouts  1.77 us (2%)
    pallas_call x1, Pallas kernels, shards(): pl.pallas_call(kernel, out_shape=jax.ShapeDtypeStruct((tok_rows, features...  113 us

profile of v3, /device:TPU:0, one launch (start us, length us, event | category | flops | bytes accessed | tf_op | source)
XLA Modules:
  0.0 114.6 jit_solution(16743962650122240306)
XLA Ops:
  0.0 112.9 %shard_map.55 = bf16[64,3072]{1,0:T(8,128)(2,1)} custom-call(bf16[64,3072]{1,0:T(8,128)(2,1)} %tok_ref.1, s32[2,64]{1,0:T(2,128)} %bitcast.6, f32[2,64]{1,0:T(2,128)} %bitcast.7, bf16[1024,3072]{1,0:T(8,128)(2,1)} %bitcast.4, bf16[1024,3072]{1,0:T(8,128)(2,1)} %bitcast.5), custom_call_target="tpu_custom_call" | custom-call | flops 28991029248 | bytes 18874368 | tf_op jit(solution)/shard_map/pallas_call | solution.py:414
  112.9 1.8 %copy.7 = bf16[64,3072]{1,0:T(8,128)(2,1)} copy(bf16[64,3072]{1,0:T(8,128)(2,1)} %shard_map.55) | data formatting | bytes 786432

commit v4 on v3

--- a/solution.py
+++ b/solution.py
@@ -14,19 +14,19 @@
     (1, 3), (3, 1), (2, 0), (0, 2),
     (1, 0), (3, 0), (0, 1), (0, 3),
 )
-PIECE_ORDER = (0, 2, 1, 3)
+PIECE_ORDER = (0, 4, 1, 5, 2, 6, 3, 7)
 PEERS = len(OFFSETS)
 BLOCKS = 8
 TILE = 16
 EXTRA = 2
 GROUPS = TILE // EXTRA
-PIECES = 4
+PIECES = 8
 PIECE = PEERS // PIECES * TILE
 PLANE = PEERS * TILE
 REST = PEERS * EXTRA
 ROWS = PLANE + REST
 TILE_N = 1024
-WAY_A, WAY_B = (0, 1), (2, 3)
+WAY_A, WAY_B = (0, 1, 2, 3), (4, 5, 6, 7)
 FIRST_ROWS = (((0,), (0,)), ((), ()))
 LAST_COLS = (((1,), (1,)), ((), ()))
 
@@ -196,8 +196,10 @@
     on_up = {k: link(xp_at(3, k), xp_at(2, k), sem_fs.at[k], sem_fr.at[k], above) for k in WAY_B}
 
     slots = [own_slots, None, None, None]
-    for k, j in zip(PIECE_ORDER, (1, 3, 0, 2)):
-        if j:
+    for k, j in zip(PIECE_ORDER, (1, None, 3, None, 0, None, 2, None)):
+        if j is None:
+            pass
+        elif j:
             meta_copies[4 - j].wait_recv()
             tok_copies[4 - j].wait_recv()
             slots[j] = slots_of(meta_v[j])
@@ -210,9 +212,12 @@
             else:
                 out_copies[r - 1].wait_recv()
         (down_copies if k in WAY_A else up_copies)[k].start()
-    for a, b in zip(WAY_A, WAY_B):
-        down_copies[b].start()
-        up_copies[a].start()
+        if k == 0:
+            up_copies[0].start()
+    for k in WAY_B:
+        down_copies[k].start()
+    for k in WAY_A[1:]:
+        up_copies[k].start()
 
     parts = ((xp_v, yp_v, fold_p, cols_p), (xz_v, yz_v, fold_z, cols_z))
 
@@ -290,13 +295,13 @@
     own_down.wait()
     twin_copies[1].wait_recv()
     enter(1)
-    for a, b in zip(WAY_A, WAY_B):
-        to_above[a].start()
-        to_below[b].start()
     return_z(1)
     for a, b in zip(WAY_A, WAY_B):
         down_copies[b].wait_recv()
         up_copies[a].wait_recv()
+    for a, b in zip(WAY_A, WAY_B):
+        to_above[a].start()
+        to_below[b].start()
     enter(3)
     return_z(3)
     for a, b in zip(WAY_A, WAY_B):
@@ -358,14 +363,15 @@
             total += other[piece(k), :].astype(F32)
         target[j, piece(k), :] = total.astype(BF16)
 
-    for a, b, j in zip(WAY_A, WAY_B, (3, 2)):
+    for a, b, j in zip(WAY_A, WAY_B, (None, 3, None, 2)):
         far_below[a].wait_recv()
         add_into(yp_v, 3, a, (far_v,))
         to_below[a].start()
         far_above[b].wait_recv()
         add_into(yp_v, 3, b, (far_v,))
         to_above[b].start()
-        gather_z(j)
+        if j:
+            gather_z(j)
     gather_z(0)
 
     back_keep = pltpu.make_async_copy(yp_v.at[0, at_block(0)], backp_v.at[at_block(0)], sem_self.at[1])

time: 115 us -> 110 us (0.957)
  Pallas kernels: 113 us -> 108 us
    pallas_call x1, Pallas kernels: 113 us -> 108 us  [shards(): pl.pallas_call(kernel, out_shape=jax.ShapeDtypeStruct((tok_rows, features...]
where the time goes in v4:
time: 110 us
  Pallas kernels  108 us (98%)
  local copies, waits for them, and re-layouts  1.77 us (2%)
    pallas_call x1, Pallas kernels, shards(): pl.pallas_call(kernel, out_shape=jax.ShapeDtypeStruct((tok_rows, features...  108 us

profile of v4, /device:TPU:0, one launch (start us, length us, event | category | flops | bytes accessed | tf_op | source)
XLA Modules:
  0.0 109.7 jit_solution(9453239677646398428)
XLA Ops:
  0.0 107.9 %shard_map.55 = bf16[64,3072]{1,0:T(8,128)(2,1)} custom-call(bf16[64,3072]{1,0:T(8,128)(2,1)} %tok_ref.1, s32[2,64]{1,0:T(2,128)} %bitcast.6, f32[2,64]{1,0:T(2,128)} %bitcast.7, bf16[1024,3072]{1,0:T(8,128)(2,1)} %bitcast.4, bf16[1024,3072]{1,0:T(8,128)(2,1)} %bitcast.5), custom_call_target="tpu_custom_call" | custom-call | flops 28991029248 | bytes 18874368 | tf_op jit(solution)/shard_map/pallas_call | solution.py:420
  107.9 1.8 %copy.7 = bf16[64,3072]{1,0:T(8,128)(2,1)} copy(bf16[64,3072]{1,0:T(8,128)(2,1)} %shard_map.55) | data formatting | bytes 786432

commit v5 on v4

--- a/solution.py
+++ b/solution.py
@@ -79,7 +79,8 @@
     above, below, twin = planes[1], planes[3], device(0, 0, 0, 1)
 
     barrier = pltpu.get_barrier_semaphore()
-    greeted = peers[1:] + planes[1:] + [twin]
+    farthest = sorted(range(1, PEERS), key=lambda r: -sum(min(d, 4 - d) for d in OFFSETS[r]))
+    greeted = [planes[2]] + [peers[r] for r in farthest] + [above, below, twin]
     for other in greeted:
         pl.semaphore_signal(barrier, inc=1, device_id=other, device_id_type=MESH)
 
@@ -137,12 +138,17 @@
     pl.semaphore_wait(barrier, len(greeted))
 
     tok_copies = [None] + [
-        link(tok_ref.at[:, pl.ds(cols_p, cols_z)], tok_v.at[4 - j], sem_ts.at[j], sem_tr.at[4 - j], planes[j]) for j in (1, 2, 3)]
+        link(tok_ref.at[:, pl.ds(cols_p, cols_z)], tok_v.at[4 - j], sem_ts.at[j], sem_tr.at[4 - j], planes[j]) if j != 2 else None
+        for j in (1, 2, 3)]
+    half = cols_z // 2
+    tok_on = {j: link(tok_v.at[j, :, pl.ds(at, half)], tok_v.at[2, :, pl.ds(at, half)], sem_ts.at[j - 1], sem_tr.at[j - 1], planes[4 - j])
+              for j, at in ((1, 0), (3, half))}
     meta_copies = [None] + [
         link(meta_ref, meta_v.at[4 - j], sem_ms.at[j], sem_mr.at[4 - j], planes[j]) for j in (1, 2, 3)]
     for j in (1, 3, 2):
         meta_copies[j].start()
-        tok_copies[j].start()
+        if j != 2:
+            tok_copies[j].start()
 
     def from_block(r):
         dx, dy = OFFSETS[r]
@@ -201,7 +207,12 @@
             pass
         elif j:
             meta_copies[4 - j].wait_recv()
-            tok_copies[4 - j].wait_recv()
+            if j == 2:
+                tok_on[1].wait_recv()
+                tok_on[3].wait_recv()
+            else:
+                tok_copies[4 - j].wait_recv()
+                tok_on[j].start()
             slots[j] = slots_of(meta_v[j])
             spread_z(j, picks_of(slots[j]), tok_v.at[j], 0)
         else:
@@ -328,20 +339,24 @@
         high = full.astype(BF16).astype(F32)
         return jnp.where(is_high, high, full - high)
 
-    def combine(found, meta, src, cols, put):
+    def weights_of(found, meta):
+        rest = weigh(found, meta, TILE + within % EXTRA)
+        return weigh(found, meta, within).astype(BF16), [
+            jnp.where(within // EXTRA == g, rest, 0.0).astype(BF16) for g in range(GROUPS)]
+
+    def combine(weights, src, cols, put):
+        main, rest = weights
         fold = cols // GROUPS
-        main = weigh(found, meta, within).astype(BF16)
-        rest = weigh(found, meta, TILE + within % EXTRA)
         for g in range(GROUPS):
             at = slice(g * fold, (g + 1) * fold)
             both = lax.dot_general(main, src[:, at], FIRST_ROWS, preferred_element_type=F32)
-            both += lax.dot_general(jnp.where(within // EXTRA == g, rest, 0.0).astype(BF16), src[:, cols:],
-                                    FIRST_ROWS, preferred_element_type=F32)
+            both += lax.dot_general(rest[g], src[:, cols:], FIRST_ROWS, preferred_element_type=F32)
             put(at, both[:tok_rows] + both[tok_rows:])
 
     part_copies = [None] + [link(part_v.at[j], got_v.at[j], sem_gs.at[j], sem_gr.at[j], planes[j]) for j in (1, 2, 3)]
 
     def gather_z(j):
+        weights = own_weights if j == 0 else weights_of(slots[j], meta_v[j])
         backz_keep[j].wait()
         for copy in backz_copies[j]:
             copy.wait_recv()
@@ -349,7 +364,7 @@
         def put(at, value):
             part_v[j, :, at] = value.astype(BF16)
 
-        combine(slots[j], meta_ref[...] if j == 0 else meta_v[j], backz_v.at[j], cols_z, put)
+        combine(weights, backz_v.at[j], cols_z, put)
         if j:
             part_copies[j].start()
 
@@ -372,7 +387,7 @@
         to_above[b].start()
         if j:
             gather_z(j)
-    gather_z(0)
+    own_weights = weights_of(own_slots, meta_ref[...])
 
     back_keep = pltpu.make_async_copy(yp_v.at[0, at_block(0)], backp_v.at[at_block(0)], sem_self.at[1])
     back_copies = [
@@ -383,6 +398,8 @@
         add_into(yp_v, 0, k, (from_up, from_down))
         for r in offsets_of(k):
             (back_keep if r == 0 else back_copies[r - 1]).start()
+        if k == PIECE_ORDER[PIECES // 2 - 1]:
+            gather_z(0)
 
     for j in (1, 2, 3):
         part_copies[j].wait_recv()
@@ -398,10 +415,11 @@
     def put_out(at, value):
         out_ref[:, at] = value.astype(BF16)
 
-    combine(own_slots, meta_ref[...], backp_v, cols_p, put_out)
+    combine(own_weights, backp_v, cols_p, put_out)
 
     onward = [way[k] for way in (on_up, on_down, far_below, far_above) for k in sorted(way)]
-    for copy in (out_copies + twin_copies + up_copies + down_copies + to_above + to_below + onward + back_copies + tok_copies[1:] + meta_copies[1:] + part_copies[1:]):
+    for copy in (out_copies + twin_copies + up_copies + down_copies + to_above + to_below + onward + back_copies
+                 + [tok_copies[1], tok_copies[3], tok_on[1], tok_on[3]] + meta_copies[1:] + part_copies[1:]):
         copy.wait_send()
     for j in range(4):
         for copy in out_z[j] + backz_copies[j]:

time: 110 us -> 109 us (level)
  no operation moved by 1% of the time
where the time goes in v5:
time: 109 us
  Pallas kernels  108 us (99%)
  local copies, waits for them, and re-layouts  1.77 us (2%)
    pallas_call x1, Pallas kernels, shards(): pl.pallas_call(kernel, out_shape=jax.ShapeDtypeStruct((tok_rows, features...  108 us

profile of v5, /device:TPU:0, one launch (start us, length us, event | category | flops | bytes accessed | tf_op | source)
XLA Modules:
  0.0 109.3 jit_solution(6927313646981649576)
XLA Ops:
  0.0 107.6 %shard_map.55 = bf16[64,3072]{1,0:T(8,128)(2,1)} custom-call(bf16[64,3072]{1,0:T(8,128)(2,1)} %tok_ref.1, s32[2,64]{1,0:T(2,128)} %bitcast.6, f32[2,64]{1,0:T(2,128)} %bitcast.7, bf16[1024,3072]{1,0:T(8,128)(2,1)} %bitcast.4, bf16[1024,3072]{1,0:T(8,128)(2,1)} %bitcast.5), custom_call_target="tpu_custom_call" | custom-call | flops 28991029248 | bytes 18874368 | tf_op jit(solution)/shard_map/pallas_call | solution.py:438
  107.6 1.8 %copy.7 = bf16[64,3072]{1,0:T(8,128)(2,1)} copy(bf16[64,3072]{1,0:T(8,128)(2,1)} %shard_map.55) | data formatting | bytes 786432
